TPU v7x, 32 devices: a whole 2x2x4 slice. The times are simulated.
32 devices in a mesh: section: 4 (over y, x), tensor: 8 (over z, core).
Axes of the slice: x: 2, y: 2, z: 4, core: 2. Of those that a mesh axis runs over, the one named last changes fastest.
Arguments:
- queries: bfloat16 [4, 512, 8192], P('section', None, 'tensor'), may hold values from -20 to 20
- key_rows: bfloat16 [4, 512, 1024], P('section'), may hold values from -6 to 6
- value_rows: bfloat16 [4, 512, 1024], P('section'), may hold values from -6 to 6
- out_grad: bfloat16 [4, 512, 8192], P('section', None, 'tensor'), may hold values from -24 to 24
- layer_input: bfloat16 [4, 512, 8192], P('section', 'tensor'), may hold values from -64 to 64
- query_weight: bfloat16 [4, 8192, 8192], P('section', None, 'tensor'), may hold values from -0.0625 to 0.0625
- dion_basis: float32 [4, 8192, 256], P('section', 'tensor'), may hold values from -0.0625 to 0.0625
- lengths: int32 [4, 3], P('section'), may hold values from 1 to 256, 512 in all within a row
Outputs:
- upstream: bfloat16 [4, 512, 8192], P('section', 'tensor')
- left_factor: float32 [4, 8192, 256], P('section', 'tensor')
- right_factor: float32 [4, 8192, 256], P('section', 'tensor')
Inputs may be any that keep to these rules, and one draw needn't show every extreme that they name: For each section the lengths of the prompt, the chosen and the rejected response, in that order, summing to 512.
All inputs are finite; a program needn't handle non-finite values.
Results may differ from a plain program's by a relative error of at most 0.022.
Values may be sent and summed in bfloat16 or wider, within the bound.
A program may use at most 128 MiB of HBM per device.

v0:
```python
import functools
import math

import jax
import jax.numpy as jnp
from jax import lax
from jax.experimental import pallas as pl
from jax.experimental.pallas import tpu as pltpu
from jax.sharding import PartitionSpec as P

D = 8192
HD = 128
GROUP = 8
MESH = pl.DeviceIdType.MESH

rope_base = 500000.0
highest = lax.Precision.HIGHEST
f32 = jnp.float32
bf16 = jnp.bfloat16


def shifted(value, axis, steps):
    count = lax.axis_size(axis)
    first, last = (max(0, -steps), min(count, count - steps))
    return lax.ppermute(value, axis, [(source, source + steps) for source in range(first, last)])


def tree_layout(lengths_row, token_count):
    token_ids = jnp.arange(token_count, dtype=jnp.int32)
    bound_one = lengths_row[0]
    bound_two = lengths_row[0] + lengths_row[1]
    positions = jnp.where(token_ids < bound_two, token_ids, token_ids - lengths_row[1]).astype(f32)
    row_ids = token_ids[:, None]
    col_ids = token_ids[None, :]
    crossed = (row_ids >= bound_two) & (col_ids >= bound_one) & (col_ids < bound_two)
    visible = (col_ids <= row_ids) & jnp.logical_not(crossed)
    bias = jnp.where(visible, 0.0, -1e30).astype(f32)
    freq_ids = jnp.arange(HD // 2, dtype=f32)
    inverse = jnp.exp(-math.log(rope_base) * 2.0 * freq_ids / HD)
    angles = positions[:, None] * inverse[None, :]
    scale = 1.0 / math.sqrt(HD)
    cosine, sine = jnp.cos(angles) * scale, jnp.sin(angles) * scale
    return (
        bias,
        jnp.concatenate([cosine, cosine], axis=-1),
        jnp.concatenate([sine, -sine], axis=-1),
    )


def nt(a, b):
    return lax.dot_general(a, b, (((1,), (1,)), ((), ())), preferred_element_type=f32)


def attend(q_ref, g_ref, k_ref, v_ref, bias_ref, cos_ref, sin_ref, out_ref):
    tokens, width = q_ref.shape
    half = tokens // 2
    scale = 1.0 / math.sqrt(HD)

    def head(h, carry):
        lanes = pl.ds(pl.multiple_of(h * HD, HD), HD)
        for part in range(2):
            rows, seen = pl.ds(part * half, half), pl.ds(0, (part + 1) * half)
            keys, values = k_ref[seen, :], v_ref[seen, :]
            q, g = q_ref[rows, lanes], g_ref[rows, lanes]
            scores = nt(q, keys) * scale + bias_ref[rows, seen]
            exps = jnp.exp(scores - jnp.max(scores, axis=-1, keepdims=True))
            weights = exps * (1.0 / jnp.sum(exps, axis=-1, keepdims=True))
            outputs = jnp.dot(weights.astype(bf16), values, preferred_element_type=f32)
            out_dot = jnp.sum(g.astype(f32) * outputs, axis=-1, keepdims=True)
            score_grad = (weights * (nt(g, values) - out_dot)).astype(bf16)
            rotated = jnp.dot(score_grad, keys, preferred_element_type=f32)
            swapped = jnp.concatenate([rotated[:, HD // 2 :], rotated[:, : HD // 2]], axis=-1)
            out_ref[rows, lanes] = (
                rotated * cos_ref[rows, :] + swapped * sin_ref[rows, :]
            ).astype(bf16)
        return carry

    lax.fori_loop(0, width // HD, head, 0)


def attention_kernel(
    n, q_ref, g_ref, k_ref, v_ref, bias_ref, cos_ref, sin_ref, x_ref, out_ref, cols_ref,
    send_sem, recv_sem,
):
    me = lax.axis_index("tensor")
    rows = x_ref.shape[0]
    width = x_ref.shape[1] // n
    barrier = pltpu.get_barrier_semaphore()
    for step in range(1, n):
        pl.semaphore_signal(
            barrier, inc=1, device_id={"tensor": lax.rem(me + step, n)}, device_id_type=MESH
        )
    pl.semaphore_wait(barrier, n - 1)
    mine = pl.ds(pl.multiple_of(me * rows, rows), rows)
    copies = []
    for step in range(1, n):
        peer = lax.rem(me + step, n)
        copies.append(
            pltpu.make_async_remote_copy(
                src_ref=x_ref.at[:, pl.ds(pl.multiple_of(peer * width, width), width)],
                dst_ref=cols_ref.at[mine, :],
                send_sem=send_sem.at[step],
                recv_sem=recv_sem.at[step],
                device_id={"tensor": peer},
                device_id_type=MESH,
            )
        )
    for copy in copies:
        copy.start()
    own = pltpu.make_async_copy(
        x_ref.at[:, pl.ds(pl.multiple_of(me * width, width), width)],
        cols_ref.at[mine, :],
        send_sem.at[0],
    )
    own.start()
    attend(q_ref, g_ref, k_ref, v_ref, bias_ref, cos_ref, sin_ref, out_ref)
    own.wait()
    for copy in copies:
        copy.wait()


def attention(n, q, g, k, v, bias, cosine, sine, x):
    tokens, width = q.shape
    vmem = pl.BlockSpec(memory_space=pltpu.VMEM)
    return pl.pallas_call(
        functools.partial(attention_kernel, n),
        out_shape=(
            jax.ShapeDtypeStruct((tokens, width), bf16),
            jax.ShapeDtypeStruct((tokens, x.shape[1] // n), bf16),
        ),
        in_specs=[vmem] * 8,
        out_specs=(vmem, vmem),
        scratch_shapes=[pltpu.SemaphoreType.DMA((n,)), pltpu.SemaphoreType.DMA((n,))],
        compiler_params=pltpu.CompilerParams(
            collective_id=0, has_side_effects=True, vmem_limit_bytes=40 * 2**20
        ),
        cost_estimate=pl.CostEstimate(
            flops=8 * tokens * tokens * width, bytes_accessed=8 * tokens * width,
            transcendentals=tokens * tokens * width // HD,
        ),
    )(q, g, k, v, bias, cosine, sine, x)


BLOCK = 64


def hdot(a, b, dims):
    return lax.dot_general(a, b, (dims, ((), ())), precision=highest, preferred_element_type=f32)


def diagonal_inverse(block):
    size = block.shape[0]
    rows = lax.broadcasted_iota(jnp.int32, (size, size), 0)
    lanes = lax.broadcasted_iota(jnp.int32, (size, size), 1)
    wide = jnp.concatenate([block, (rows == lanes).astype(f32)], axis=1)
    row_ids = lax.broadcasted_iota(jnp.int32, (size, 1), 0)
    for k in range(size - 1):
        factor = wide[:, k : k + 1] * (1.0 / wide[k : k + 1, k : k + 1])
        wide = wide - jnp.where(row_ids > k, factor, 0.0) * wide[k : k + 1, :]
    diagonal = jnp.sum(jnp.where(rows == lanes, wide[:, :size], 0.0), axis=1, keepdims=True)
    return wide[:, size:] * lax.rsqrt(diagonal)


def factor_inverse(gram_ref, inv_ref):
    rank = gram_ref.shape[0]
    rows = lax.broadcasted_iota(jnp.int32, (rank, rank), 0)
    lanes = lax.broadcasted_iota(jnp.int32, (rank, rank), 1)
    inv_ref[...] = (rows == lanes).astype(f32)
    for start in range(0, rank, BLOCK):
        end = start + BLOCK
        inner = diagonal_inverse(gram_ref[start:end, start:end])
        top = hdot(inner, inv_ref[start:end, :], ((1,), (0,)))
        inv_ref[start:end, :] = top
        if end < rank:
            panel = hdot(gram_ref[end:, start:end], inner, ((1,), (1,)))
            gram_ref[end:, end:] = gram_ref[end:, end:] - hdot(panel, panel, ((1,), (1,)))
            inv_ref[end:, :] = inv_ref[end:, :] - hdot(panel, top, ((1,), (0,)))


def finish_kernel(proj_ref, mixed_ref, raw_ref, grad_ref, left_ref, right_ref, gram, inv):
    gram[...] = hdot(proj_ref[...], mixed_ref[...], ((0,), (0,)))
    factor_inverse(gram, inv)
    left_ref[...] = hdot(raw_ref[...], inv[...], ((1,), (1,))) * math.sqrt(D)
    orth = hdot(mixed_ref[...], inv[...], ((1,), (1,)))
    high = orth.astype(bf16)
    low = (orth - high.astype(f32)).astype(bf16)
    grad = grad_ref[...]
    dims = (((0,), (0,)), ((), ()))
    right_ref[...] = lax.dot_general(
        grad, high, dims, preferred_element_type=f32
    ) + lax.dot_general(grad, low, dims, preferred_element_type=f32)


def finish(projected, mixed, raw, grad):
    rank = projected.shape[1]
    vmem = pl.BlockSpec(memory_space=pltpu.VMEM)
    return pl.pallas_call(
        finish_kernel,
        out_shape=(
            jax.ShapeDtypeStruct(raw.shape, f32),
            jax.ShapeDtypeStruct((grad.shape[1], rank), f32),
        ),
        in_specs=[vmem] * 4,
        out_specs=(vmem, vmem),
        scratch_shapes=[pltpu.VMEM((rank, rank), f32), pltpu.VMEM((rank, rank), f32)],
        compiler_params=pltpu.CompilerParams(vmem_limit_bytes=40 * 2**20),
        cost_estimate=pl.CostEstimate(flops=10**10, bytes_accessed=10**7, transcendentals=0),
    )(projected, mixed, raw, grad)


def pieces(wide, count=3):
    out = []
    for _ in range(count):
        out.append(wide.astype(bf16))
        wide = wide - out[-1].astype(f32)
    return out


def exact_dot(low, wide, dims, count=3):
    return sum(
        lax.dot_general(low, piece, (dims, ((), ())), preferred_element_type=f32)
        for piece in pieces(wide, count)
    )


def local(queries, key_rows, value_rows, out_grad, layer_input, query_weight, dion_basis, lengths):
    token_count = queries.shape[1]
    local_heads = queries.shape[2] // HD
    tensor_count = lax.axis_size("tensor")
    tensor_index = lax.axis_index("tensor")
    bias, cosine, sine = tree_layout(lengths[0], token_count)
    group_head = tensor_index * local_heads // GROUP
    key_block = lax.dynamic_slice_in_dim(key_rows[0], group_head * HD, HD, 1)
    value_block = lax.dynamic_slice_in_dim(value_rows[0], group_head * HD, HD, 1)
    query_grad, columns = attention(
        tensor_count, queries[0], out_grad[0], key_block, value_block, bias, cosine, sine,
        layer_input[0],
    )
    projected = lax.psum(exact_dot(query_grad, dion_basis[0], ((1,), (0,))), "tensor")
    layer_grad = lax.psum_scatter(
        nt(query_grad, query_weight[0]).astype(bf16), "tensor", scatter_dimension=0, tiled=True
    )
    upstream = shifted(layer_grad, "section", -1)
    left_raw = exact_dot(columns, projected, ((0,), (0,)))
    mixed = lax.psum(exact_dot(columns, left_raw, ((1,), (0,))), "tensor")
    left_factor, right_factor = finish(projected, mixed, left_raw, query_grad)
    return (upstream[None], left_factor[None], right_factor[None])


def solution(mesh):
    placed = (
        P("section", None, "tensor"),
        P("section", None, None),
        P("section", None, None),
        P("section", None, "tensor"),
        P("section", "tensor", None),
        P("section", None, "tensor"),
        P("section", "tensor", None),
        P("section", None),
    )
    return jax.shard_map(
        local,
        mesh=mesh,
        in_specs=placed,
        out_specs=(
            P("section", "tensor", None),
            P("section", "tensor", None),
            P("section", "tensor", None),
        ),
        check_vma=False,
    )
```

profile of v0, /device:TPU:0, one launch (start us, length us, event | category | flops | bytes accessed | tf_op | source)
XLA Modules:
  0.0 294.2 jit_solution(9267095250585577278)
XLA Ops:
  7.2 0.0 copy-start.5
  7.2 0.0 all-reduce.3.cloned.1.call-start
  7.2 1.3 fusion.22
  8.6 0.6 iota_compare_fusion.2
  10.5 0.7 select_convert_fusion
  11.2 1.0 fusion.19
  12.2 1.0 dynamic-slice_bitcast_fusion
  13.2 0.2 pad_maximum_fusion
  13.4 0.2 fusion.6.bias_ref
  13.7 0.0 copy-start.1
  13.7 1.2 copy-done.1
  14.9 0.0 copy-start.2
  14.9 1.2 copy-done.2
  16.1 0.0 copy-start.3
  16.1 1.2 copy-done.3
  17.4 22.6 %shard_map.103 = (bf16[512,1024]{1,0:T(8,128)(2,1)S(1)}, bf16[512,1024]{1,0:T(8,128)(2,1)S(1)}) custom-call(bf16[512,1024]{1,0:T(8,128)(2,1)S(1)} %bitcast.52, bf16[512,1024]{1,0:T(8,128)(2,1)S(1)} %bitcast.53, bf16[512,128]{1,0:T(8,128)(2,1)S(1)} %get-tuple-element.17.k_ref, bf16[512,128]{1,0:T(8,128)(2,1)S(1)} %get-tuple-element.16.v_ref, ...), custom_call_target="tpu_custom_call" | custom-call | flops 2147483648 | bytes 4194304 | tf_op jit(solution)/shard_map/pallas_call | solution.py:125
  40.0 1.7 fusion.23
  41.7 1.7 convolution_add_fusion.5
  43.3 0.0 copy-done.5
  43.4 1.3 convolution_add_fusion.4
  44.6 0.0 all-reduce.3.cloned.1.call-update
  44.6 0.0 reduce-scatter.2.cloned.1.call-start
  44.7 29.7 %fusion.2 = bf16[512,8192]{1,0:T(8,128)(2,1)} fusion(bf16[512,1024]{1,0:T(8,128)(2,1)S(1)} %get-tuple-element.7.grad_ref, bf16[1,8192,1024]{2,1,0:T(8,128)(2,1)} %param.13), kind=kOutput, calls=%fused_computation.2 | convolution fusion | flops 8594128896 | bytes 26214400 | tf_op jit(solution)/shard_map/dot_general | solution.py:51
  74.3 0.0 reduce-scatter.2.cloned.1.call-update
  74.4 0.0 all-reduce.5.cloned.1.call-start
  74.4 32.6 %all-reduce.3.cloned.1.call-done.proj_ref = f32[512,256]{1,0:T(8,128)} async-done(((f32[512,256]{1,0:T(8,128)}), f32[512,256]{1,0:T(8,128)}) %all-reduce.3.cloned.1.call-update) | async-done | bytes 524304 | tf_op jit(solution)/shard_map/psum | solution.py:239
  107.0 1.5 fusion.15
  108.5 1.7 convolution_add_fusion.1
  110.2 1.7 convolution_add_fusion.raw_ref
  111.9 0.4 fusion.8
  112.4 0.4 convolution_add_fusion.3
  112.8 1.2 convolution_add_fusion.2
  114.1 0.0 all-reduce.5.cloned.1.call-update
  114.1 83.9 %reduce-scatter.2.cloned.1.call-done = bf16[64,8192]{1,0:T(8,128)(2,1)} async-done(((bf16[512,8192]{1,0:T(8,128)(2,1)}), bf16[64,8192]{1,0:T(8,128)(2,1)}) %reduce-scatter.2.cloned.1.call-update) | async-done | bytes 1048592 | tf_op jit(solution)/shard_map/reduce_scatter | solution.py:240
  198.0 1.5 collective-permute-start
  199.5 56.1 %all-reduce.5.cloned.1.call-done.mixed_ref = f32[512,256]{1,0:T(8,128)} async-done(((f32[512,256]{1,0:T(8,128)}), f32[512,256]{1,0:T(8,128)}) %all-reduce.5.cloned.1.call-update) | async-done | bytes 524304 | tf_op jit(solution)/shard_map/psum | solution.py:245
  255.6 0.0 copy-start
  255.6 1.0 copy-done
  256.6 0.0 copy-start.4
  256.6 1.0 copy-done.4
  257.6 27.7 %shard_map.104 = (f32[1024,256]{1,0:T(8,128)}, f32[1024,256]{1,0:T(8,128)}) custom-call(f32[512,256]{1,0:T(8,128)S(1)} %copy-done, f32[512,256]{1,0:T(8,128)S(1)} %copy-done.4, f32[1024,256]{1,0:T(8,128)S(1)} %convolution_add_fusion.raw_ref, bf16[512,1024]{1,0:T(8,128)(2,1)S(1)} %get-tuple-element.7.grad_ref), custom_call_target="tpu_custom_call" | custom-call | flops 10000000000 | bytes 10000000 | tf_op jit(solution)/shard_map/pallas_call | solution.py:197
  285.4 0.0 collective-permute-done
  285.4 2.3 copy.14
  (2 shorter events, 0.0 us)
Async XLA Ops:
  7.2 36.2 %copy-start.5 = (f32[1,1024,256]{2,1,0:T(8,128)S(1)}, f32[1,1024,256]{2,1,0:T(8,128)}, u32[]{:S(2)}) copy-start(f32[1,1024,256]{2,1,0:T(8,128)} %param.14) | copy-start | bytes 3145732
  7.2 99.8 %all-reduce.3.cloned.1.call-start = ((), (), s32[]{:S(2)}) async-start(), calls=%async_computation.2 | async-start | bytes 1048576 | tf_op jit(solution)/shard_map/psum | solution.py:239
  13.7 1.2 copy-start.1
  14.9 1.2 copy-start.2
  16.1 1.2 copy-start.3
  44.6 153.4 %reduce-scatter.2.cloned.1.call-start = ((), (), s32[]{:S(2)}) async-start(), calls=%async_computation.1 | async-start | bytes 9437184 | tf_op jit(solution)/shard_map/reduce_scatter | solution.py:240
  74.4 181.2 %all-reduce.5.cloned.1.call-start = ((), (), s32[]{:S(2)}) async-start(), calls=%async_computation.3 | async-start | bytes 1048576 | tf_op jit(solution)/shard_map/psum | solution.py:245
  198.0 87.4 %collective-permute-start = (bf16[64,8192]{1,0:T(8,128)(2,1)}, bf16[64,8192]{1,0:T(8,128)(2,1)}, u32[]{:S(2)}, u32[]{:S(2)}) collective-permute-start(bf16[64,8192]{1,0:T(8,128)(2,1)} %reduce-scatter.2.cloned.1.call-done), channel_id=1, source_target_pairs={{8,0},{16,8},{24,16},{9,1},{17,9},{25,17},{10,2},{18,10},{26,18},{... | collective-permute-start | bytes 3145736 | tf_op jit(solution)/shard_map/ppermute | solution.py:25
  255.6 1.0 copy-start
  256.6 1.0 copy-start.4
Sparse Core Ops, SparseCore 0:
  44.8 62.1 all-reduce.2
  109.4 88.5 reduce-scatter.1
  201.0 54.4 all-reduce.4
where the time goes:
time: 295 us; the launch traced here: 294 us
  waiting for transfers between devices  173 us (59%)
  Pallas kernels  50.4 us (17%)
  matrix products  41.3 us (14%)
  between operations  15.2 us (5%)
  local copies, waits for them, and re-layouts  10.3 us (3%)
    reduce_scatter x1, waiting for transfers between devices, local(): lax.psum_scatter(nt(query_grad, query_weight[0]).astype(bf16), 'tensor',...  83.9 us
    psum x1, waiting for transfers between devices, local(): mixed = lax.psum(exact_dot(columns, left_raw, ((1,), (0,))), 'tensor')  56.1 us
    psum x1, waiting for transfers between devices, local(): lax.psum(exact_dot(query_grad, dion_basis[0], ((1,), (0,))), 'tensor')  32.6 us
    dot_general x1, matrix products, nt(): lax.dot_general(a, b, (((1,), (1,)), ((), ())), preferred_element_type=f32)  29.7 us
    pallas_call x1, Pallas kernels, finish(): pl.pallas_call(finish_kernel, out_shape=(jax.ShapeDtypeStruct(raw.shape,...  27.7 us
    pallas_call x1, Pallas kernels, attention(): pl.pallas_call(functools.partial(attention_kernel, n), out_shape=(jax.Sha...  22.6 us
    dot_general x9, matrix products, exact_dot(): lax.dot_general(low, piece, (dims, ((), ())), preferred_element_type=f32)  11.6 us
    unnamed x13, local copies, waits for them, and re-layouts  8.02 us
  transfers between devices with their start and end apart: 4, of which 3 were waited for; matrix products, arithmetic and copies ran while one was open for 12% of the time, Pallas kernels for 9%

commit v1 on v0

--- a/solution.py
+++ b/solution.py
@@ -17,12 +17,6 @@
 highest = lax.Precision.HIGHEST
 f32 = jnp.float32
 bf16 = jnp.bfloat16
-
-
-def shifted(value, axis, steps):
-    count = lax.axis_size(axis)
-    first, last = (max(0, -steps), min(count, count - steps))
-    return lax.ppermute(value, axis, [(source, source + steps) for source in range(first, last)])
 
 
 def tree_layout(lengths_row, token_count):
@@ -161,7 +155,7 @@
     return wide[:, size:] * lax.rsqrt(diagonal)
 
 
-def factor_inverse(gram_ref, inv_ref):
+def factor_inverse(gram_ref, inv_ref, between):
     rank = gram_ref.shape[0]
     rows = lax.broadcasted_iota(jnp.int32, (rank, rank), 0)
     lanes = lax.broadcasted_iota(jnp.int32, (rank, rank), 1)
@@ -175,37 +169,7 @@
             panel = hdot(gram_ref[end:, start:end], inner, ((1,), (1,)))
             gram_ref[end:, end:] = gram_ref[end:, end:] - hdot(panel, panel, ((1,), (1,)))
             inv_ref[end:, :] = inv_ref[end:, :] - hdot(panel, top, ((1,), (0,)))
-
-
-def finish_kernel(proj_ref, mixed_ref, raw_ref, grad_ref, left_ref, right_ref, gram, inv):
-    gram[...] = hdot(proj_ref[...], mixed_ref[...], ((0,), (0,)))
-    factor_inverse(gram, inv)
-    left_ref[...] = hdot(raw_ref[...], inv[...], ((1,), (1,))) * math.sqrt(D)
-    orth = hdot(mixed_ref[...], inv[...], ((1,), (1,)))
-    high = orth.astype(bf16)
-    low = (orth - high.astype(f32)).astype(bf16)
-    grad = grad_ref[...]
-    dims = (((0,), (0,)), ((), ()))
-    right_ref[...] = lax.dot_general(
-        grad, high, dims, preferred_element_type=f32
-    ) + lax.dot_general(grad, low, dims, preferred_element_type=f32)
-
-
-def finish(projected, mixed, raw, grad):
-    rank = projected.shape[1]
-    vmem = pl.BlockSpec(memory_space=pltpu.VMEM)
-    return pl.pallas_call(
-        finish_kernel,
-        out_shape=(
-            jax.ShapeDtypeStruct(raw.shape, f32),
-            jax.ShapeDtypeStruct((grad.shape[1], rank), f32),
-        ),
-        in_specs=[vmem] * 4,
-        out_specs=(vmem, vmem),
-        scratch_shapes=[pltpu.VMEM((rank, rank), f32), pltpu.VMEM((rank, rank), f32)],
-        compiler_params=pltpu.CompilerParams(vmem_limit_bytes=40 * 2**20),
-        cost_estimate=pl.CostEstimate(flops=10**10, bytes_accessed=10**7, transcendentals=0),
-    )(projected, mixed, raw, grad)
+        between(end // BLOCK)
 
 
 def pieces(wide, count=3):
@@ -221,6 +185,308 @@
         lax.dot_general(low, piece, (dims, ((), ())), preferred_element_type=f32)
         for piece in pieces(wide, count)
     )
+
+
+CHUNKS = 8
+
+
+def dion_kernel(
+    n, sections, grad_ref, weight_ref, cols_ref, basis_ref, up_ref, left_ref, right_ref,
+    wbuf, part, sib, from_left, from_right, gram, inv, raw,
+    p_part, p_sib, p_recv, p_full, m_part, m_sib, m_recv, m_full,
+    w_sem, pair_sem, right_sem, left_sem, shift_sem, p_sem, m_sem,
+):
+    chips = n // 2
+    me = lax.axis_index("tensor")
+    section = lax.axis_index("section")
+    chip, core = me // 2, lax.rem(me, 2)
+    other = 1 - core
+    tokens = grad_ref.shape[0]
+    rows = tokens // n
+    rank = basis_ref.shape[1]
+    chunk = wbuf.shape[1]
+    sibling = {"tensor": chip * 2 + other}
+    first, last = section == 0, section == sections - 1
+
+    def load(j):
+        return pltpu.make_async_copy(
+            weight_ref.at[pl.ds(j * chunk, chunk), :], wbuf.at[j], w_sem.at[j]
+        )
+
+    for j in range(CHUNKS):
+        load(j).start()
+
+    def remote(src, dst, sems, index, device):
+        return pltpu.make_async_remote_copy(
+            src_ref=src, dst_ref=dst, send_sem=sems.at[(0, *index)], recv_sem=sems.at[(1, *index)],
+            device_id=device, device_id_type=MESH,
+        )
+
+    barrier = pltpu.get_barrier_semaphore()
+
+    def greet(device):
+        pl.semaphore_signal(barrier, inc=1, device_id=device, device_id_type=MESH)
+
+    greet(sibling)
+    for step in range(1, chips):
+        greet({"tensor": lax.rem(chip + step, chips) * 2 + core})
+
+    greet({"section": lax.rem(section + sections - 1, sections)})
+    greet({"section": lax.rem(section + 1, sections)})
+    pl.semaphore_wait(barrier, chips + 2)
+
+    class Reduce:
+        def __init__(self, part, sib, recv, full, sems):
+            self.part, self.sib, self.recv, self.full, self.sems = part, sib, recv, full, sems
+
+        def one(self):
+            return remote(self.part.at[:, other], self.sib, self.sems, (0,), sibling)
+
+        def two(self, step):
+            peer = lax.rem(chip + step, chips)
+            return remote(
+                self.part.at[peer, core], self.recv.at[step], self.sems, (step,),
+                {"tensor": peer * 2 + core},
+            )
+
+        def three(self, step):
+            peer = lax.rem(chip + step, chips)
+            slot = self.full.at[chip, core]
+            return remote(slot, slot, self.sems, (chips + step,), {"tensor": peer * 2 + core})
+
+        def four(self):
+            slot = self.full.at[:, core]
+            return remote(slot, slot, self.sems, (chips,), sibling)
+
+        def start(self, value):
+            self.part[...] = value.reshape(chips, 2, rows, rank)
+            self.one().start()
+
+        def scatter(self):
+            self.one().wait_recv()
+            self.part[:, core] = self.part[:, core] + self.sib[...]
+            for step in range(1, chips):
+                self.two(step).start()
+
+        def gather(self):
+            total = self.part[chip, core]
+            for step in range(1, chips):
+                self.two(step).wait_recv()
+                total = total + self.recv[step]
+            self.full[chip, core] = total
+            for step in range(1, chips):
+                self.three(step).start()
+
+        def pair(self):
+            for step in range(1, chips):
+                self.three(step).wait_recv()
+            self.four().start()
+
+        def result(self):
+            self.four().wait()
+            self.one().wait_send()
+            for step in range(1, chips):
+                self.two(step).wait_send()
+                self.three(step).wait_send()
+            return self.full[...].reshape(tokens, rank)
+
+    def send_pair(j):
+        return remote(part.at[j, :, other], sib.at[j], pair_sem, (j,), sibling)
+
+    def send_right(j, b):
+        return remote(
+            part.at[j, b, core], from_left.at[j, b], right_sem, (j, b),
+            {"tensor": lax.rem(chip + 1, chips) * 2 + core},
+        )
+
+    def send_left(j, b):
+        return remote(
+            part.at[j, b, core], from_right.at[j, b], left_sem, (j, b),
+            {"tensor": lax.rem(chip + chips - 1, chips) * 2 + core},
+        )
+
+    def send_shift(j):
+        return remote(
+            part.at[j, chip, core], up_ref.at[:, pl.ds(j * chunk, chunk)], shift_sem, (j,),
+            {"section": lax.rem(section + sections - 1, sections)},
+        )
+
+    def multiply(j):
+        load(j).wait()
+
+        def tile(t, carry):
+            lanes = pl.ds(pl.multiple_of(t * 256, 256), 256)
+            out = nt(grad_ref[...], wbuf[j, lanes, :]).astype(bf16)
+            part[j, :, :, :, lanes] = out.reshape(chips, 2, rows, 256)
+            return carry
+
+        lax.fori_loop(0, chunk // 256, tile, 0)
+        send_pair(j).start()
+
+    def pair_sum(j):
+        send_pair(j).wait_recv()
+        part[j, :, core] = (part[j, :, core].astype(f32) + sib[j].astype(f32)).astype(bf16)
+
+        @pl.when(chip == 0)
+        def _():
+            for b in range(chips - 1, 0, -1):
+                send_right(j, b).start()
+
+        @pl.when(chip == chips - 1)
+        def _():
+            for b in range(chips - 1):
+                send_left(j, b).start()
+
+    def add_to(j, b, arrived):
+        part[j, b, core] = (
+            part[j, b, core].astype(f32) + arrived[j, b].astype(f32)
+        ).astype(bf16)
+
+    def hop(j):
+        for b in range(chips - 1, 0, -1):
+
+            @pl.when((chip > 0) & (chip < b))
+            def _():
+                send_right(j, b).wait_recv()
+                add_to(j, b, from_left)
+                send_right(j, b).start()
+
+        for b in range(chips - 1):
+
+            @pl.when((chip < chips - 1) & (chip > b))
+            def _():
+                send_left(j, b).wait_recv()
+                add_to(j, b, from_right)
+                send_left(j, b).start()
+
+        for b in range(chips):
+
+            @pl.when(chip == b)
+            def _():
+                if b > 0:
+                    send_right(j, b).wait_recv()
+                    add_to(j, b, from_left)
+                if b < chips - 1:
+                    send_left(j, b).wait_recv()
+                    add_to(j, b, from_right)
+
+        @pl.when(jnp.logical_not(first))
+        def _():
+            send_shift(j).start()
+
+    projected_sum = Reduce(p_part, p_sib, p_recv, p_full, p_sem)
+    mixed_sum = Reduce(m_part, m_sib, m_recv, m_full, m_sem)
+    projected_sum.start(exact_dot(grad_ref[...], basis_ref[...], ((1,), (0,))))
+    multiply(0)
+    projected_sum.scatter()
+    multiply(1)
+    pair_sum(0)
+    projected_sum.gather()
+    multiply(2)
+    pair_sum(1)
+    projected_sum.pair()
+    multiply(3)
+    pair_sum(2)
+    projected = projected_sum.result()
+    raw[...] = exact_dot(cols_ref[...], projected, ((0,), (0,)))
+    mixed_sum.start(exact_dot(cols_ref[...], raw[...], ((1,), (0,))))
+    multiply(4)
+    pair_sum(3)
+    mixed_sum.scatter()
+    multiply(5)
+    pair_sum(4)
+    mixed_sum.gather()
+    multiply(6)
+    pair_sum(5)
+    mixed_sum.pair()
+    multiply(7)
+    pair_sum(6)
+    pair_sum(7)
+    hop(0)
+    mixed = mixed_sum.result()
+    gram[...] = hdot(p_full[...].reshape(tokens, rank), mixed, ((0,), (0,)))
+    factor_inverse(gram, inv, hop)
+    left_ref[...] = hdot(raw[...], inv[...], ((1,), (1,))) * math.sqrt(D)
+    orth = hdot(m_full[...].reshape(tokens, rank), inv[...], ((1,), (1,)))
+    right_ref[...] = exact_dot(grad_ref[...], orth, ((0,), (0,)), 2)
+    for j in range(rank // BLOCK + 1, CHUNKS):
+        hop(j)
+
+    @pl.when(last)
+    def _():
+        up_ref[...] = jnp.zeros_like(up_ref)
+
+    for j in range(CHUNKS):
+
+        @pl.when(jnp.logical_not(last))
+        def _():
+            send_shift(j).wait_recv()
+
+        @pl.when(jnp.logical_not(first))
+        def _():
+            send_shift(j).wait_send()
+
+        send_pair(j).wait_send()
+        for b in range(chips):
+
+            @pl.when(chip < b)
+            def _():
+                send_right(j, b).wait_send()
+
+            @pl.when(chip > b)
+            def _():
+                send_left(j, b).wait_send()
+
+
+def dion(n, sections, grad, weight, columns, basis):
+    tokens, width = grad.shape
+    rank = basis.shape[1]
+    chips, rows = n // 2, tokens // n
+    depth = weight.shape[0]
+    chunk = depth // CHUNKS
+    vmem = pl.BlockSpec(memory_space=pltpu.VMEM)
+    reduce_scratch = [
+        pltpu.VMEM((chips, 2, rows, rank), f32),
+        pltpu.VMEM((chips, rows, rank), f32),
+        pltpu.VMEM((chips, rows, rank), f32),
+        pltpu.VMEM((chips, 2, rows, rank), f32),
+    ]
+    dma = pltpu.SemaphoreType.DMA
+    return pl.pallas_call(
+        functools.partial(dion_kernel, n, sections),
+        out_shape=(
+            jax.ShapeDtypeStruct((rows, depth), bf16),
+            jax.ShapeDtypeStruct((columns.shape[1], rank), f32),
+            jax.ShapeDtypeStruct((width, rank), f32),
+        ),
+        in_specs=[vmem, pl.BlockSpec(memory_space=pl.ANY), vmem, vmem],
+        out_specs=(vmem, vmem, vmem),
+        scratch_shapes=[
+            pltpu.VMEM((CHUNKS, chunk, width), bf16),
+            pltpu.VMEM((CHUNKS, chips, 2, rows, chunk), bf16),
+            pltpu.VMEM((CHUNKS, chips, rows, chunk), bf16),
+            pltpu.VMEM((CHUNKS, chips, rows, chunk), bf16),
+            pltpu.VMEM((CHUNKS, chips, rows, chunk), bf16),
+            pltpu.VMEM((rank, rank), f32),
+            pltpu.VMEM((rank, rank), f32),
+            pltpu.VMEM((columns.shape[1], rank), f32),
+            *reduce_scratch,
+            *reduce_scratch,
+            dma((CHUNKS,)),
+            dma((2, CHUNKS)),
+            dma((2, CHUNKS, chips)),
+            dma((2, CHUNKS, chips)),
+            dma((2, CHUNKS)),
+            dma((2, 2 * chips)),
+            dma((2, 2 * chips)),
+        ],
+        compiler_params=pltpu.CompilerParams(
+            collective_id=1, has_side_effects=True, vmem_limit_bytes=60 * 2**20
+        ),
+        cost_estimate=pl.CostEstimate(
+            flops=2 * tokens * width * depth, bytes_accessed=2 * width * depth, transcendentals=0
+        ),
+    )(grad, weight, columns, basis)
 
 
 def local(queries, key_rows, value_rows, out_grad, layer_input, query_weight, dion_basis, lengths):
@@ -236,14 +502,9 @@
         tensor_count, queries[0], out_grad[0], key_block, value_block, bias, cosine, sine,
         layer_input[0],
     )
-    projected = lax.psum(exact_dot(query_grad, dion_basis[0], ((1,), (0,))), "tensor")
-    layer_grad = lax.psum_scatter(
-        nt(query_grad, query_weight[0]).astype(bf16), "tensor", scatter_dimension=0, tiled=True
-    )
-    upstream = shifted(layer_grad, "section", -1)
-    left_raw = exact_dot(columns, projected, ((0,), (0,)))
-    mixed = lax.psum(exact_dot(columns, left_raw, ((1,), (0,))), "tensor")
-    left_factor, right_factor = finish(projected, mixed, left_raw, query_grad)
+    upstream, left_factor, right_factor = dion(
+        tensor_count, lax.axis_size("section"), query_grad, query_weight[0], columns, dion_basis[0]
+    )
     return (upstream[None], left_factor[None], right_factor[None])
 
 

time: 295 us -> 239 us (0.81)
  waiting for transfers between devices: 173 us -> 0 us
  Pallas kernels: 50.4 us -> 219 us
  matrix products: 41.3 us -> 0 us
  between operations: 15.2 us -> 2.03 us
  local copies, waits for them, and re-layouts: 10.3 us -> 14.7 us
    pallas_call x1, Pallas kernels: 27.7 us -> 196 us  [dion(): pl.pallas_call(functools.partial(dion_kernel, n, sections), out_shape=(ja...]
    psum x2 -> x0, waiting for transfers between devices: 88.7 us -> none  [the longest x1 56.1 us: local(): mixed = lax.psum(exact_dot(columns, left_raw, ((1,), (0,))), 'tensor')]
    reduce_scatter x1 -> x0, waiting for transfers between devices: 83.9 us -> none  [local(): lax.psum_scatter(nt(query_grad, query_weight[0]).astype(bf16), 'tensor',...]
    dot_general x10 -> x0, matrix products: 41.3 us -> none  [the longest x1 29.7 us: nt(): lax.dot_general(a, b, (((1,), (1,)), ((), ())), preferred_element_type=f32)]
    unnamed x13, local copies, waits for them, and re-layouts: 8.02 us -> 12.4 us
  transfers between devices with their start and end apart: 4 -> 0, of which waited for: 3 -> 0; matrix products, arithmetic and copies ran while one was open for 12% -> 0% of each run, Pallas kernels for 9% -> 0%
where the time goes in v1:
time: 239 us; the launch traced here: 238 us
  Pallas kernels  219 us (92%)
  local copies, waits for them, and re-layouts  14.7 us (6%)
  other arithmetic  2.76 us (1%)
    pallas_call x1, Pallas kernels, dion(): pl.pallas_call(functools.partial(dion_kernel, n, sections), out_shape=(ja...  196 us
    pallas_call x1, Pallas kernels, attention(): pl.pallas_call(functools.partial(attention_kernel, n), out_shape=(jax.Sha...  22.6 us
    unnamed x13, local copies, waits for them, and re-layouts  12.4 us

profile of v1, /device:TPU:0, one launch (start us, length us, event | category | flops | bytes accessed | tf_op | source)
XLA Modules:
  0.0 238.3 jit_solution(7755892468526827488)
XLA Ops:
  0.7 1.3 fusion.5
  3.3 0.7 iota_compare_fusion.2
  3.9 0.7 select_convert_fusion
  4.6 1.0 dynamic-slice_bitcast_fusion
  5.6 1.0 fusion.3
  6.6 0.2 pad_maximum_fusion
  6.8 0.2 fusion.1.bias_ref
  7.1 0.0 copy-start
  7.1 1.2 copy-done
  8.3 0.0 copy-start.1
  8.3 1.2 copy-done.1
  9.5 0.0 copy-start.2
  9.5 1.2 copy-done.2
  10.7 22.6 %shard_map.103 = (bf16[512,1024]{1,0:T(8,128)(2,1)S(1)}, bf16[512,1024]{1,0:T(8,128)(2,1)S(1)}) custom-call(bf16[512,1024]{1,0:T(8,128)(2,1)S(1)} %bitcast.14, bf16[512,1024]{1,0:T(8,128)(2,1)S(1)} %bitcast.15, bf16[512,128]{1,0:T(8,128)(2,1)S(1)} %get-tuple-element.19.k_ref, bf16[512,128]{1,0:T(8,128)(2,1)S(1)} %get-tuple-element.18.v_ref, ...), custom_call_target="tpu_custom_call" | custom-call | flops 2147483648 | bytes 4194304 | tf_op jit(solution)/shard_map/pallas_call | solution.py:119
  33.4 0.0 copy-start.3
  33.4 1.0 copy-done.3
  34.4 0.0 copy-start.4
  34.4 1.0 copy-done.4
  35.3 196.2 %shard_map.104 = (bf16[64,8192]{1,0:T(8,128)(2,1)}, f32[1024,256]{1,0:T(8,128)}, f32[1024,256]{1,0:T(8,128)}) custom-call(bf16[512,1024]{1,0:T(8,128)(2,1)} %copy-done.3, bf16[8192,1024]{1,0:T(8,128)(2,1)} %bitcast.20, bf16[512,1024]{1,0:T(8,128)(2,1)} %copy-done.4, f32[1024,256]{1,0:T(8,128)} %bitcast.21), custom_call_target="tpu_custom_call" | custom-call | flops 8589934592 | bytes 16777216 | tf_op jit(solution)/shard_map/pallas_call | solution.py:455
  231.5 2.3 copy.14
  233.8 2.3 copy.15
  236.0 2.3 copy.16
  (2 shorter events, 0.0 us)
Async XLA Ops:
  7.1 1.2 copy-start
  8.3 1.2 copy-start.1
  9.5 1.2 copy-start.2
  33.4 1.0 copy-start.3
  34.4 1.0 copy-start.4

commit v2 on v1

--- a/solution.py
+++ b/solution.py
@@ -327,6 +327,7 @@
         send_pair(j).wait_recv()
         part[j, :, core] = (part[j, :, core].astype(f32) + sib[j].astype(f32)).astype(bf16)
 
+    def inject(j):
         @pl.when(chip == 0)
         def _():
             for b in range(chips - 1, 0, -1):
@@ -382,6 +383,7 @@
     multiply(1)
     pair_sum(0)
     projected_sum.gather()
+    inject(0)
     multiply(2)
     pair_sum(1)
     projected_sum.pair()
@@ -396,12 +398,17 @@
     multiply(5)
     pair_sum(4)
     mixed_sum.gather()
+    for j in range(1, 5):
+        inject(j)
     multiply(6)
     pair_sum(5)
+    inject(5)
     mixed_sum.pair()
     multiply(7)
     pair_sum(6)
+    inject(6)
     pair_sum(7)
+    inject(7)
     hop(0)
     mixed = mixed_sum.result()
     gram[...] = hdot(p_full[...].reshape(tokens, rank), mixed, ((0,), (0,)))

time: 239 us -> 218 us (0.912)
  Pallas kernels: 219 us -> 198 us
    pallas_call x1, Pallas kernels: 196 us -> 175 us  [dion(): pl.pallas_call(functools.partial(dion_kernel, n, sections), out_shape=(ja...]
where the time goes in v2:
time: 218 us; the launch traced here: 217 us
  Pallas kernels  198 us (91%)
  local copies, waits for them, and re-layouts  14.7 us (7%)
  other arithmetic  2.76 us (1%)
    pallas_call x1, Pallas kernels, dion(): pl.pallas_call(functools.partial(dion_kernel, n, sections), out_shape=(ja...  175 us
    pallas_call x1, Pallas kernels, attention(): pl.pallas_call(functools.partial(attention_kernel, n), out_shape=(jax.Sha...  22.6 us
    unnamed x13, local copies, waits for them, and re-layouts  12.4 us

profile of v2, /device:TPU:0, one launch (start us, length us, event | category | flops | bytes accessed | tf_op | source)
XLA Modules:
  0.0 217.3 jit_solution(14346833344985210373)
XLA Ops:
  0.7 1.3 fusion.5
  3.3 0.7 iota_compare_fusion.2
  3.9 0.7 select_convert_fusion
  4.6 1.0 dynamic-slice_bitcast_fusion
  5.6 1.0 fusion.3
  6.6 0.2 pad_maximum_fusion
  6.8 0.2 fusion.1.bias_ref
  7.1 0.0 copy-start
  7.1 1.2 copy-done
  8.3 0.0 copy-start.1
  8.3 1.2 copy-done.1
  9.5 0.0 copy-start.2
  9.5 1.2 copy-done.2
  10.7 22.6 %shard_map.103 = (bf16[512,1024]{1,0:T(8,128)(2,1)S(1)}, bf16[512,1024]{1,0:T(8,128)(2,1)S(1)}) custom-call(bf16[512,1024]{1,0:T(8,128)(2,1)S(1)} %bitcast.14, bf16[512,1024]{1,0:T(8,128)(2,1)S(1)} %bitcast.15, bf16[512,128]{1,0:T(8,128)(2,1)S(1)} %get-tuple-element.19.k_ref, bf16[512,128]{1,0:T(8,128)(2,1)S(1)} %get-tuple-element.18.v_ref, ...), custom_call_target="tpu_custom_call" | custom-call | flops 2147483648 | bytes 4194304 | tf_op jit(solution)/shard_map/pallas_call | solution.py:119
  33.4 0.0 copy-start.3
  33.4 1.0 copy-done.3
  34.4 0.0 copy-start.4
  34.4 1.0 copy-done.4
  35.3 175.2 %shard_map.104 = (bf16[64,8192]{1,0:T(8,128)(2,1)}, f32[1024,256]{1,0:T(8,128)}, f32[1024,256]{1,0:T(8,128)}) custom-call(bf16[512,1024]{1,0:T(8,128)(2,1)} %copy-done.3, bf16[8192,1024]{1,0:T(8,128)(2,1)} %bitcast.20, bf16[512,1024]{1,0:T(8,128)(2,1)} %copy-done.4, f32[1024,256]{1,0:T(8,128)} %bitcast.21), custom_call_target="tpu_custom_call" | custom-call | flops 8589934592 | bytes 16777216 | tf_op jit(solution)/shard_map/pallas_call | solution.py:462
  210.6 2.3 %copy.14 = bf16[1,64,8192]{2,1,0:T(8,128)(2,1)} copy(bf16[1,64,8192]{2,1,0:T(8,128)(2,1)} %bitcast.19) | data formatting | bytes 2097152
  212.8 2.3 %copy.15 = f32[1,1024,256]{2,1,0:T(8,128)} copy(f32[1,1024,256]{2,1,0:T(8,128)} %bitcast.18) | data formatting | bytes 2097152
  215.1 2.3 %copy.16 = f32[1,1024,256]{2,1,0:T(8,128)} copy(f32[1,1024,256]{2,1,0:T(8,128)} %bitcast.17) | data formatting | bytes 2097152
  (2 shorter events, 0.0 us)
Async XLA Ops:
  7.1 1.2 copy-start
  8.3 1.2 copy-start.1
  9.5 1.2 copy-start.2
  33.4 1.0 copy-start.3
  34.4 1.0 copy-start.4
